TPU v7x, 32 devices: a whole 2x2x4 slice. The times are simulated.
32 devices in a mesh: panel: 16 (over z, y, core), rep: 2 (over x).
Axes of the slice: x: 2, y: 2, z: 4, core: 2. Of those that a mesh axis runs over, the one named last changes fastest.
Arguments:
- x_src: bfloat16 [2048, 128], P('panel'), may hold values from -6 to 6
- x_dst: bfloat16 [16384, 128], P(('panel', 'rep')), may hold values from -6 to 6
- weight: bfloat16 [128, 512], replicated, may hold values from -0.5 to 0.5
- att_src: float32 [8, 64], replicated, may hold values from -0.75 to 0.75
- att_dst: float32 [8, 64], replicated, may hold values from -0.75 to 0.75
- grad_out: bfloat16 [16384, 512], P(('panel', 'rep')), may hold values from -6 to 6
- block_rows: int32 [512], P(('panel', 'rep')), may hold values from 0 to 3, as said below
- block_cols: int32 [512], P(('panel', 'rep')), may hold values from 0 to 15
- block_masks: int32 [512, 128, 128], P(('panel', 'rep')), may hold values from 0 to 1, as said below
- block_counts: int32 [32], P(('panel', 'rep')), may hold values from 2 to 16, as said below
Outputs:
- grad_src: float32 [2048, 128], P('panel')
- grad_dst: float32 [16384, 128], P(('panel', 'rep'))
- grad_weight: float32 [128, 512], replicated
- grad_att_src: float32 [8, 64], replicated
- grad_att_dst: float32 [8, 64], replicated
Inputs may be any that keep to these rules, and one draw needn't show every extreme that they name: `block_counts`: live block slots of one device; at least one device has exactly 16. The pairs of block_rows and block_cols within one device's 16 slots are distinct. `block_masks`: slots at or after a device's count of live blocks hold only zeros.
All inputs are finite; a program needn't handle non-finite values.
Results may differ from a plain program's by a relative error of at most 0.012.
The roundings to bfloat16 on the way count: a program that leaves them out, or rounds other values in their place, can miss the bound.
Values may be sent and summed in bfloat16 or wider, within the bound.
A program may use at most 128 MiB of HBM per device.

v0:
```python
import math

import jax
import jax.numpy as jnp
from jax import lax
from jax.sharding import PartitionSpec as P

HIGHEST_PRECISION = lax.Precision.HIGHEST


def smooth_leaky(values):
    return 0.2 * values + 0.8 * jax.nn.softplus(values)


def smooth_slope(values):
    return 0.2 + 0.8 * jax.nn.sigmoid(values)


def shards(
    x_src,
    x_dst,
    weight,
    att_src,
    att_dst,
    grad_out,
    block_rows,
    block_cols,
    block_masks,
    block_counts,
):
    num_heads, head_dim = att_src.shape
    model_width = weight.shape[1]
    block_size = block_masks.shape[1]
    dest_count = x_dst.shape[0]
    source_local = x_src.shape[0]
    slot_count = block_rows.shape[0]
    proj_own = jnp.dot(x_src, weight, preferred_element_type=jnp.float32).astype(jnp.bfloat16)
    proj_all = lax.all_gather(proj_own, "panel", axis=0, tiled=True)
    source_total = proj_all.shape[0]
    dest_blocks = dest_count // block_size
    source_blocks = source_total // block_size
    source_feats = proj_all.reshape(source_total, num_heads, head_dim)
    score_src = jnp.einsum(
        "jhk,hk->hj", source_feats.astype(jnp.float32), att_src, precision=HIGHEST_PRECISION
    )
    proj_dst = jnp.dot(x_dst, weight, preferred_element_type=jnp.float32).astype(jnp.bfloat16)
    feats = proj_dst.reshape(dest_count, num_heads, head_dim)
    feats_wide = feats.astype(jnp.float32)
    score_d = jnp.einsum("ihk,hk->hi", feats_wide, att_dst, precision=HIGHEST_PRECISION)
    score_own = jnp.einsum("ihk,hk->hi", feats_wide, att_src, precision=HIGHEST_PRECISION)
    cotan = grad_out.reshape(dest_count, num_heads, head_dim)
    cotan_wide = cotan.astype(jnp.float32)
    live_count = block_counts[0]
    score_d_blocks = score_d.reshape(num_heads, dest_blocks, block_size)
    score_src_blocks = score_src.reshape(num_heads, source_blocks, block_size)
    source_row_blocks = source_feats.reshape(source_blocks, block_size, num_heads, head_dim)
    cotan_blocks = cotan.reshape(dest_blocks, block_size, num_heads, head_dim)
    group = math.gcd(slot_count, 16)
    groups = slot_count // group
    alive_all = (jnp.arange(slot_count, dtype=jnp.int32) < live_count).astype(jnp.float32)
    slot_inputs = (
        block_rows.reshape(groups, group),
        block_cols.reshape(groups, group),
        block_masks.reshape(groups, group, block_size, block_size),
        alive_all.reshape(groups, group),
    )

    def group_scores(rows, cols, masks, alive):
        dest_hot = (rows[:, None] == jnp.arange(dest_blocks, dtype=jnp.int32)[None, :]).astype(
            jnp.float32
        )
        source_hot = (cols[:, None] == jnp.arange(source_blocks, dtype=jnp.int32)[None, :]).astype(
            jnp.float32
        )
        score_rows = jnp.einsum(
            "gd,hdu->ghu", dest_hot, score_d_blocks, precision=HIGHEST_PRECISION
        )
        score_cols = jnp.einsum(
            "gs,hsv->ghv", source_hot, score_src_blocks, precision=HIGHEST_PRECISION
        )
        pre_score = score_rows[:, :, :, None] + score_cols[:, :, None, :]
        edge_mask = masks.astype(jnp.float32) * alive[:, None, None]
        edge_weight = jnp.exp(smooth_leaky(pre_score)) * edge_mask[:, None]
        source_rows = jnp.take(source_row_blocks, cols, axis=0)
        return (dest_hot, source_hot, pre_score, edge_weight, source_rows)

    def forward_group(carried_fwd, slot_group):
        denominator, numerator = carried_fwd
        rows, cols, masks, alive = slot_group
        dest_hot, source_hot, pre_score, edge_weight, source_rows = group_scores(
            rows, cols, masks, alive
        )
        part_num = jnp.einsum(
            "ghij,gjhk->gihk",
            edge_weight.astype(jnp.bfloat16),
            source_rows,
            preferred_element_type=jnp.float32,
        )
        denominator = denominator + jnp.einsum(
            "gd,ghi->hdi", dest_hot, edge_weight.sum(axis=3), precision=HIGHEST_PRECISION
        )
        numerator = numerator + jnp.einsum(
            "gd,gihk->dihk", dest_hot, part_num, precision=HIGHEST_PRECISION
        )
        return ((denominator, numerator), None)

    (denominator_blocks, numerator_blocks), _ = lax.scan(
        forward_group,
        (
            jnp.zeros((num_heads, dest_blocks, block_size), jnp.float32),
            jnp.zeros((dest_blocks, block_size, num_heads, head_dim), jnp.float32),
        ),
        slot_inputs,
    )
    denominator = denominator_blocks.reshape(num_heads, dest_count)
    numerator = numerator_blocks.reshape(dest_count, num_heads, head_dim)
    pre_self = score_d + score_own
    self_weight = jnp.exp(smooth_leaky(pre_self))
    denominator = denominator + self_weight
    numerator = numerator + self_weight.T[:, :, None] * feats_wide
    attended = numerator / denominator.T[:, :, None]
    centred = jnp.sum(cotan_wide * attended, axis=2).T
    denominator_full = denominator.reshape(num_heads, dest_blocks, block_size)
    centred_full = centred.reshape(num_heads, dest_blocks, block_size)

    def backward_group(carried_bwd, slot_group):
        grad_source, grad_score_src, grad_score_dst = carried_bwd
        rows, cols, masks, alive = slot_group
        dest_hot, source_hot, pre_score, edge_weight, source_rows = group_scores(
            rows, cols, masks, alive
        )
        denom_rows = jnp.einsum(
            "gd,hdi->ghi", dest_hot, denominator_full, precision=HIGHEST_PRECISION
        )
        attention = edge_weight / denom_rows[:, :, :, None]
        cotan_rows = jnp.take(cotan_blocks, rows, axis=0)
        pair_grad = jnp.einsum(
            "gihk,gjhk->ghij", cotan_rows, source_rows, preferred_element_type=jnp.float32
        )
        centred_rows = jnp.einsum(
            "gd,hdi->ghi", dest_hot, centred_full, precision=HIGHEST_PRECISION
        )
        score_grad = attention * (pair_grad - centred_rows[:, :, :, None]) * smooth_slope(pre_score)
        feat_grad = jnp.einsum(
            "ghij,gihk->gjhk",
            attention.astype(jnp.bfloat16),
            cotan_rows,
            preferred_element_type=jnp.float32,
        )
        grad_source = grad_source + jnp.einsum(
            "gs,gjhk->sjhk", source_hot, feat_grad, precision=HIGHEST_PRECISION
        )
        grad_score_src = grad_score_src + jnp.einsum(
            "gs,ghj->hsj", source_hot, score_grad.sum(axis=2), precision=HIGHEST_PRECISION
        )
        grad_score_dst = grad_score_dst + jnp.einsum(
            "gd,ghi->hdi", dest_hot, score_grad.sum(axis=3), precision=HIGHEST_PRECISION
        )
        return ((grad_source, grad_score_src, grad_score_dst), None)

    (grad_source_blocks, grad_score_src_blocks, grad_score_dst_blocks), _ = lax.scan(
        backward_group,
        (
            jnp.zeros((source_blocks, block_size, num_heads, head_dim), jnp.float32),
            jnp.zeros((num_heads, source_blocks, block_size), jnp.float32),
            jnp.zeros((num_heads, dest_blocks, block_size), jnp.float32),
        ),
        slot_inputs,
    )
    grad_source = grad_source_blocks.reshape(source_total, num_heads, head_dim)
    grad_score_src = grad_score_src_blocks.reshape(num_heads, source_total)
    grad_score_dst = grad_score_dst_blocks.reshape(num_heads, dest_count)
    self_attention = self_weight / denominator
    self_pair = jnp.sum(cotan_wide * feats_wide, axis=2).T
    self_grad = self_attention * (self_pair - centred) * smooth_slope(pre_self)
    grad_score_dst = grad_score_dst + self_grad
    grad_dest = (
        self_attention.T[:, :, None] * cotan_wide
        + self_grad.T[:, :, None] * att_src[None]
        + grad_score_dst.T[:, :, None] * att_dst[None]
    )
    grad_source = grad_source + grad_score_src.T[:, :, None] * att_src[None]
    att_src_part = jnp.einsum(
        "hj,jhk->hk", grad_score_src, source_feats.astype(jnp.float32), precision=HIGHEST_PRECISION
    ) + jnp.einsum("hi,ihk->hk", self_grad, feats_wide, precision=HIGHEST_PRECISION)
    att_dst_part = jnp.einsum("hi,ihk->hk", grad_score_dst, feats_wide, precision=HIGHEST_PRECISION)
    weight_t = weight.astype(jnp.float32).T
    source_flat = grad_source.reshape(source_total, model_width)
    dest_flat = grad_dest.reshape(dest_count, model_width)
    grad_dst = jnp.dot(dest_flat, weight_t, precision=HIGHEST_PRECISION)
    weight_part = jnp.dot(x_dst.astype(jnp.float32).T, dest_flat, precision=HIGHEST_PRECISION)
    share_rows = source_local // lax.axis_size("rep")
    share_start = lax.axis_index("rep") * share_rows
    panel_part = lax.psum_scatter(source_flat, "panel", scatter_dimension=0, tiled=True)
    panel_sum = lax.psum(panel_part, "rep")
    own_share = lax.dynamic_slice_in_dim(panel_sum, share_start, share_rows, 0)
    grad_src = jnp.dot(panel_sum, weight_t, precision=HIGHEST_PRECISION)
    own_inputs = lax.dynamic_slice_in_dim(x_src, share_start, share_rows, 0).astype(jnp.float32)
    weight_part = weight_part + jnp.dot(own_inputs.T, own_share, precision=HIGHEST_PRECISION)
    grad_weight, grad_att_src, grad_att_dst = lax.psum(
        (weight_part, att_src_part, att_dst_part), ("panel", "rep")
    )
    return (grad_src, grad_dst, grad_weight, grad_att_src, grad_att_dst)


def solution(mesh):
    return jax.shard_map(
        shards,
        mesh=mesh,
        in_specs=(
            P("panel", None),
            P(("panel", "rep"), None),
            P(),
            P(),
            P(),
            P(("panel", "rep"), None),
            P(("panel", "rep")),
            P(("panel", "rep")),
            P(("panel", "rep"), None, None),
            P(("panel", "rep")),
        ),
        out_specs=(P("panel", None), P(("panel", "rep"), None), P(), P(), P()),
        check_vma=False,
    )
```

profile of v0, /device:TPU:0, one launch (start us, length us, event | category | flops | bytes accessed | tf_op | source)
XLA Modules:
  0.0 384.7 jit_solution(17885924008814587707)
XLA Ops:
  8.1 1.6 convolution_convert_fusion.1
  9.7 1.3 copy.51
  11.0 1.8 reshape.149
  12.9 1.2 convolution_convert_fusion
  16.8 2.2 gather_fusion
  19.4 1.2 convert_multiply_fusion.2
  20.5 34.4 %all-gather.2.cloned.1.call-done = bf16[2048,512]{1,0:T(8,128)(2,1)} async-done(((bf16[128,512]{1,0:T(8,128)(2,1)}), bf16[2048,512]{1,0:T(8,128)(2,1)}) %all-gather.2.cloned.1.call-update) | async-done | bytes 2097168 | tf_op jit(solution)/shard_map/all_gather | solution.py:38
  54.9 2.9 copy.43
  59.2 9.6 %fusion.23 = f32[16,8,128]{2,1,0:T(8,128)S(1)} fusion(f32[16,128,128]{2,1,0:T(8,128)} %convert_multiply_fusion.2, f32[16,8,128]{2,1,0:T(8,128)S(1)} %copy.45, f32[16,8,128]{2,1,0:T(8,128)S(1)} %copy.42), kind=kLoop, calls=%fused_computation.33 | loop fusion | flops 25149440 | bytes 1245184 | tf_op jit(solution)/shard_map/while/body/eval_jaxpr/reduce_sum | solution.py:100
  69.0 3.7 reshape.150
  72.7 4.1 %copy.50 = bf16[16,128,8,64]{1,3,2,0:T(8,128)(2,1)S(1)} copy(bf16[16,128,8,64]{3,2,1,0:T(8,128)(2,1)} %reshape.150) | data formatting | bytes 4194304 | tf_op jit(solution)/shard_map/reshape;reshape | solution.py:56
  76.8 2.2 gather_fusion.1
  79.0 9.5 %fusion.27 = f32[16,128,8,64]{1,3,2,0:T(8,128)S(1)} fusion(f32[16,128,128]{2,1,0:T(8,128)} %convert_multiply_fusion.2, f32[16,8,128]{2,1,0:T(8,128)S(1)} %copy.45, f32[16,8,128]{2,1,0:T(8,128)S(1)} %copy.42, bf16[16,128,8,64]{1,3,2,0:T(8,128)(2,1)} %gather_fusion.1, pred[16]{0:T(512)(128)(4,1)S(1)} %get-tuple-element.104), kind=kOutput, calls=%fused_computation.35 | convolution fusion | flops 294649856 | bytes 7471120 | tf_op jit(solution)/shard_map/while/body/eval_jaxpr/ghij,gjhk->gihk/dot_general | solution.py:93
  88.5 5.0 %fusion.14 = f32[4,128,8,64]{1,0,3,2:T(4,128)} fusion(f32[16,128,8,64]{1,3,2,0:T(8,128)S(1)} %fusion.27, s32[16]{0:T(128)S(1)} %copy-done.12), kind=kOutput, calls=%fused_computation.24 | convolution fusion | flops 50331712 | bytes 5242944 | tf_op jit(solution)/shard_map/while/body/eval_jaxpr/gd,gihk->dihk/dot_general | solution.py:102
  93.5 2.6 reshape.108
  96.2 1.6 fusion.33
  98.4 11.8 %fusion.24 = f32[16,128,8,64]{1,3,2,0:T(8,128)S(1)} fusion(f32[16,8,128]{2,1,0:T(8,128)S(1)} %copy.47, f32[16,128,128]{2,1,0:T(8,128)} %convert_multiply_fusion.2, f32[16,8,128]{2,1,0:T(8,128)S(1)} %copy.45, f32[16,8,128]{2,1,0:T(8,128)S(1)} %copy.42, bf16[16,128,8,64]{1,3,2,0:T(8,128)(2,1)S(1)} %copy-done.4, pred[16]{0:T(512)(128)(4,1)S(1)} %get-tuple-element.105), kind=kOutput, calls=%fused_computation.34 | convolution fusion | flops 296747008 | bytes 7536656 | tf_op jit(solution)/shard_map/while/body/eval_jaxpr/ghij,gihk->gjhk/dot_general | solution.py:144
  110.2 15.5 %fusion.96 = (f32[16,8,128]{2,1,0:T(8,128)S(1)}, f32[16,8,128]{2,1,0:T(8,128)S(1)}) fusion(f32[16,8,128]{2,1,0:T(8,128)S(1)} %copy.53, bf16[16,128,8,64]{1,3,2,0:T(8,128)(2,1)S(1)} %copy-done.5, pred[16]{0:T(512)(128)(4,1)S(1)} %get-tuple-element.104, bf16[16,128,8,64]{1,3,2,0:T(8,128)(2,1)S(1)} %copy-done.4, pred[16]{0:T(512)(128)(4,1)S(1)} %get-tuple-element.105, ...), kind=kOutput, calls=%fused_computation.128 | convolution fusion | flops 316637184 | bytes 5636128 | tf_op jit(solution)/shard_map/while/body/eval_jaxpr/gihk,gjhk->ghij/dot_general | solution.py:137
  125.9 4.4 %fusion.16 = f32[16,128,8,64]{1,0,3,2:T(8,128)S(1)} fusion(f32[16,128,8,64]{1,3,2,0:T(8,128)S(1)} %fusion.24, s32[16]{0:T(128)S(1)} %copy-done.14), kind=kOutput, calls=%fused_computation.26 | convolution fusion | flops 201326848 | bytes 8388672 | tf_op jit(solution)/shard_map/while/body/eval_jaxpr/gs,gjhk->sjhk/dot_general | solution.py:150
  130.3 4.1 %bitcast_add_fusion = f32[2048,512]{0,1:T(8,128)} fusion(f32[64,8,16,128]{3,2,1,0:T(8,128)S(1)} %bitcast.177, f32[512]{0:T(512)S(1)} %mul.185, f32[2048,8]{0,1:T(8,128)S(1)} %bitcast.184), kind=kLoop, calls=%fused_computation.22 | loop fusion | flops 2097152 | bytes 8456192 | tf_op jit(solution)/shard_map/add | solution.py:182
  135.4 1.3 fusion.34
  136.7 2.2 fusion.59
  138.8 1.5 convolution_bitcast_fusion
  140.4 3.2 fusion.103
  143.5 62.2 %reduce-scatter.2.cloned.1.call-done = f32[128,512]{0,1:T(8,128)} async-done(((f32[2048,512]{0,1:T(8,128)}), f32[128,512]{0,1:T(8,128)}) %reduce-scatter.2.cloned.1.call-update) | async-done | bytes 262160 | tf_op jit(solution)/shard_map/reduce_scatter | solution.py:194
  205.8 1.5 fusion.57
  208.1 39.7 %all-reduce = (f32[8,64]{1,0:T(8,128)}, f32[8,64]{1,0:T(8,128)}) all-reduce(f32[8,64]{1,0:T(8,128)S(1)} %add.168, f32[8,64]{1,0:T(8,128)S(1)} %bitcast.198), channel_id=1, replica_groups=mesh['panel'=16,'rep'=2] {'panel','rep'}, use_global_device_ids=true, to_apply=%region_8.10 | all-reduce | flops 1024 | bytes 8192 | tf_op jit(solution)/shard_map/psum | solution.py:200
  247.8 1.7 fusion.102
  249.5 2.0 convolution_add_fusion
  251.5 2.0 fusion.101
  253.5 122.9 %all-reduce.6.cloned.1.call-done = f32[128,512]{0,1:T(8,128)} async-done(((f32[128,512]{0,1:T(8,128)}), f32[128,512]{0,1:T(8,128)}) %all-reduce.6.cloned.1.call-update) | async-done | bytes 262160 | tf_op jit(solution)/shard_map/psum | solution.py:200
  376.4 1.8 copy.57
  (73 shorter events, 7.3 us)
Async XLA Ops:
  7.2 0.9 copy-start
  7.2 8.0 %copy-start.12 = (s32[16]{0:T(128)S(1)}, s32[16]{0:T(128)}, u32[]{:S(2)}) copy-start(s32[16]{0:T(128)} %param.18) | copy-start | bytes 196
  7.2 9.5 %copy-start.11 = (f32[8,64]{1,0:T(8,128)S(1)}, f32[8,64]{1,0:T(8,128)}, u32[]{:S(2)}) copy-start(f32[8,64]{1,0:T(8,128)} %param.15) | copy-start | bytes 6148
  7.2 47.7 %all-gather.2.cloned.1.call-start = ((), (), s32[]{:S(2)}) async-start(), calls=%async_computation.1 | async-start | bytes 2228224 | tf_op jit(solution)/shard_map/all_gather | solution.py:38
  9.7 196.1 %reduce-scatter.2.cloned.1.call-start = ((), (), s32[]{:S(2)}) async-start(), calls=%async_computation.2 | async-start | bytes 4456448 | tf_op jit(solution)/shard_map/reduce_scatter | solution.py:194
  11.0 85.2 %copy-start.7 = (bf16[512,512]{0,1:T(8,128)(2,1)}, bf16[512,512]{0,1:T(8,128)(2,1)S(1)}, u32[]{:S(2)}) copy-start(bf16[512,512]{0,1:T(8,128)(2,1)S(1)} %copy.51) | copy-start | bytes 1572868
  14.1 82.1 %copy-start.6 = (bf16[512,512]{0,1:T(8,128)(2,1)}, bf16[512,512]{0,1:T(8,128)(2,1)S(1)}, u32[]{:S(2)}) copy-start(bf16[512,512]{0,1:T(8,128)(2,1)S(1)} %convolution_convert_fusion) | copy-start | bytes 1572868
  16.8 2.2 copy-start.14
  16.8 2.5 copy-start.8
  57.8 1.3 copy-start.2
  59.2 9.9 %copy-start.1 = (bf16[2048,512]{1,0:T(8,128)(2,1)S(1)}, bf16[2048,512]{1,0:T(8,128)(2,1)}, u32[]{:S(2)}) copy-start(bf16[2048,512]{1,0:T(8,128)(2,1)} %all-gather.2.cloned.1.call-done) | copy-start | bytes 6291460
  88.5 9.8 %copy-start.4 = (bf16[16,128,8,64]{1,3,2,0:T(8,128)(2,1)S(1)}, bf16[16,128,8,64]{1,3,2,0:T(8,128)(2,1)}, u32[]{:S(2)}) copy-start(bf16[16,128,8,64]{1,3,2,0:T(8,128)(2,1)} %gather_fusion) | copy-start | bytes 6291460
  98.3 11.8 %copy-start.5 = (bf16[16,128,8,64]{1,3,2,0:T(8,128)(2,1)S(1)}, bf16[16,128,8,64]{1,3,2,0:T(8,128)(2,1)}, u32[]{:S(2)}) copy-start(bf16[16,128,8,64]{1,3,2,0:T(8,128)(2,1)} %gather_fusion.1) | copy-start | bytes 6291460
  98.4 11.8 %copy-start.9 = (f32[16,128,128]{2,1,0:T(8,128)S(1)}, f32[16,128,128]{2,1,0:T(8,128)}, u32[]{:S(2)}) copy-start(f32[16,128,128]{2,1,0:T(8,128)} %convert_multiply_fusion.2) | copy-start | bytes 3145732
  125.8 4.5 %copy-start.10 = (f32[8,128,16]{1,2,0:T(8,128)}, f32[8,128,16]{1,2,0:T(8,128)S(1)}, u32[]{:S(2)}) copy-start(f32[8,128,16]{1,2,0:T(8,128)S(1)} %fusion.42) | copy-start | bytes 196612
  134.4 0.7 copy-start.13
  134.4 5.9 %copy-start.3 = (bf16[2048,512]{0,1:T(8,128)(2,1)S(1)}, bf16[2048,512]{0,1:T(8,128)(2,1)}, u32[]{:S(2)}) copy-start(bf16[2048,512]{0,1:T(8,128)(2,1)} %copy-done.2) | copy-start | bytes 6291460
  134.5 115.0 %all-reduce.4.cloned.1.call-start = ((), (), s32[]{:S(2)}) async-start(), calls=%async_computation.3 | async-start | bytes 524288 | tf_op jit(solution)/shard_map/psum | solution.py:195
  205.8 170.6 %all-reduce.6.cloned.1.call-start = ((), (), s32[]{:S(2)}) async-start(), calls=%async_computation.4 | async-start | bytes 524288 | tf_op jit(solution)/shard_map/psum | solution.py:200
Sparse Core Ops, SparseCore 0:
  10.8 44.0 all-gather.1
  134.6 71.1 reduce-scatter.1
  208.1 22.4 all-reduce.3
  251.6 124.6 all-reduce.5
where the time goes:
time: 386 us; the launch traced here: 385 us
  waiting for transfers between devices  220 us (57%)
  matrix products  66.7 us (17%)
  blocking collectives  39.7 us (10%)
  local copies, waits for them, and re-layouts  25.1 us (7%)
  other arithmetic  18.6 us (5%)
  between operations  14.8 us (4%)
    psum x1, waiting for transfers between devices, shards(): lax.psum((weight_part, att_src_part, att_dst_part), ('panel', 'rep'))  123 us
    reduce_scatter x1, waiting for transfers between devices, shards(): lax.psum_scatter(source_flat, 'panel', scatter_dimension=0, tiled=True)  62.2 us
    psum x1, blocking collectives, shards(): lax.psum((weight_part, att_src_part, att_dst_part), ('panel', 'rep'))  39.7 us
    all_gather x1, waiting for transfers between devices, shards(): proj_all = lax.all_gather(proj_own, 'panel', axis=0, tiled=True)  34.4 us
    dot_general x1, matrix products, backward_group(): jnp.einsum('gihk,gjhk->ghij', cotan_rows, source_rows, preferred_element_...  15.5 us
    dot_general x1, matrix products, backward_group(): jnp.einsum('ghij,gihk->gjhk', attention.astype(jnp.bfloat16), cotan_rows,...  11.8 us
    reduce_sum x1, other arithmetic, forward_group(): edge_weight.sum(axis=3)  9.62 us
    dot_general x1, matrix products, forward_group(): jnp.einsum('ghij,gjhk->gihk', edge_weight.astype(jnp.bfloat16), source_ro...  9.53 us
  transfers between devices with their start and end apart: 4, of which 3 were waited for; matrix products, arithmetic and copies ran while one was open for 6% of the time, Pallas kernels for 0%

commit v1 on v0

v1 whole, which is shorter than its diff:
```python
import jax
import jax.numpy as jnp
from jax import lax
from jax.experimental import pallas as pl
from jax.experimental.pallas import tpu as pltpu
from jax.sharding import PartitionSpec as P

F32 = jnp.float32
BF16 = jnp.bfloat16
MESH = pl.DeviceIdType.MESH
LANES = 128


def mm(a, b, ca=1, cb=0):
    return lax.dot_general(a, b, (((ca,), (cb,)), ((), ())), preferred_element_type=F32)


def split(values, parts):
    pieces = []
    for _ in range(parts):
        piece = values.astype(BF16)
        pieces.append(piece)
        values = values - piece.astype(F32)
    return pieces


def mm_split(a, b, parts, ca=1, cb=0):
    return sum(mm(piece, b, ca, cb) for piece in split(a, parts))


def edge_terms(pre):
    small = jnp.exp(-jnp.abs(pre))
    grown = 1.0 + small
    inverse = 1.0 / grown
    sigma = 0.2 * pre + 0.8 * (jnp.maximum(pre, 0.0) + jnp.log(grown))
    sigmoid = jnp.where(pre >= 0.0, inverse, small * inverse)
    return jnp.exp(sigma), 0.2 + 0.8 * sigmoid


def iota(shape, dim):
    return lax.broadcasted_iota(jnp.int32, shape, dim)


def layer_kernel(
    rows_ref, cols_ref, count_ref, x_all_ref, x_dst_ref, weight_ref, att_src_ref, att_dst_ref,
    grad_ref, masks_ref,
    grad_dst_ref, part_src_ref, part_weight_ref, part_att_ref,
    proj_src, proj_dst, score_src, score_wide, inv_wide, weights, slopes,
    numer, denom, centre, grad_source, grad_score_src, grad_score_dst,
):
    heads, head_dim = att_src_ref.shape
    width = weight_ref.shape[1]
    pairs = width // LANES
    blk = masks_ref.shape[1]
    source_blocks = x_all_ref.shape[0] // blk
    dest = x_dst_ref.shape[0]
    count = count_ref[0]
    inputs = weight_ref.shape[0]

    lane_head = iota((heads, width), 1) // head_dim
    own = lane_head == iota((heads, width), 0)
    spread_src = jnp.where(own, jnp.concatenate([att_src_ref[...]] * heads, axis=1), 0.0)
    spread_dst = jnp.where(own, jnp.concatenate([att_dst_ref[...]] * heads, axis=1), 0.0)
    pad_rows = jnp.zeros((LANES - heads, width), F32)
    ones_heads = jnp.concatenate([jnp.where(own, 1.0, 0.0), pad_rows], axis=0).astype(BF16)
    tall_src = jnp.concatenate([spread_src, pad_rows], axis=0)
    tall_dst = jnp.concatenate([spread_dst, pad_rows], axis=0)

    for s in range(source_blocks):
        at = slice(s * blk, (s + 1) * blk)
        proj_src[at, :] = mm(x_all_ref[at, :], weight_ref[...]).astype(BF16)
    proj_dst[...] = mm(x_dst_ref[...], weight_ref[...]).astype(BF16)
    for s in range(source_blocks):
        at = slice(s * blk, (s + 1) * blk)
        stacked = jnp.concatenate([p.astype(F32) for p in split(spread_src, 3)], axis=0)
        got = mm(stacked.astype(BF16), proj_src[at, :], 1, 1)
        score_src[s] = got[:heads] + got[heads : 2 * heads] + got[2 * heads :]
    score_d = sum(mm(proj_dst[...], p, 1, 1) for p in split(tall_dst, 3))
    pre_self = score_d + sum(mm(proj_dst[...], p, 1, 1) for p in split(tall_src, 3))
    for h in range(heads):
        score_wide[h] = jnp.broadcast_to(score_d[:, h : h + 1], (dest, LANES))

    numer[...] = jnp.zeros_like(numer)
    denom[...] = jnp.zeros_like(denom)
    grad_source[...] = jnp.zeros_like(grad_source)
    grad_score_src[...] = jnp.zeros_like(grad_score_src)
    grad_score_dst[...] = jnp.zeros_like(grad_score_dst)

    low = (iota((1, LANES), 1) < head_dim).astype(F32).astype(BF16)
    high = (iota((1, LANES), 1) >= head_dim).astype(F32).astype(BF16)
    second = iota((2 * blk, LANES), 0) // blk
    lane = iota((2 * blk, LANES), 1)

    def both(values):
        return jnp.concatenate([values * low, values * high], axis=0)

    def pick(g, with_low):
        head = 2 * g + second
        hit = lane == head
        if with_low:
            hit = hit | (lane == head + heads)
        return jnp.where(hit, 1.0, 0.0)

    def forward(b, carry):
        r = pl.ds(pl.multiple_of(rows_ref[b] * blk, blk), blk)
        c = cols_ref[b]
        src = pl.ds(pl.multiple_of(c * blk, blk), blk)
        live = masks_ref[b] > 0
        scores = score_src[c]
        for g in range(pairs):
            at = slice(g * LANES, (g + 1) * LANES)
            found = []
            for h in (2 * g, 2 * g + 1):
                edge, slope = edge_terms(score_wide[h, r, :] + scores[h : h + 1, :])
                edge = jnp.where(live, edge, 0.0)
                weights[b, h] = edge
                slopes[b, h] = slope
                found.append(edge.astype(BF16))
            right = jnp.concatenate(
                [both(proj_src[src, at]), pick(g, False).astype(BF16)], axis=1
            )
            got = mm(jnp.concatenate(found, axis=1), right)
            numer[r, at] += got[:, :LANES]
            denom[r, :] += got[:, LANES:]
        return carry

    lax.fori_loop(0, count, forward, 0)

    feats = proj_dst[...].astype(F32)
    cotan = grad_ref[...].astype(F32)
    self_weight, self_slope = edge_terms(pre_self)
    inverse = 1.0 / (denom[...] + self_weight)
    total = numer[...] + mm_split(self_weight, ones_heads, 2) * feats
    narrow = mm_split(cotan * total, ones_heads, 2, 1, 1) * inverse
    lanes = iota((dest, LANES), 1)
    narrow = jnp.where(lanes < heads, narrow, 0.0)
    top = narrow.astype(BF16).astype(F32)
    centre[...] = (top + pltpu.roll(narrow - top, heads, 1)).astype(BF16)
    self_att = jnp.where(lanes < heads, self_weight * inverse, 0.0)
    self_pair = mm_split(cotan * feats, ones_heads, 2, 1, 1)
    self_grad = self_att * (self_pair - narrow) * self_slope
    for h in range(heads):
        inv_wide[h] = jnp.broadcast_to(inverse[:, h : h + 1], (dest, LANES))

    def backward(b, carry):
        r = pl.ds(pl.multiple_of(rows_ref[b] * blk, blk), blk)
        c = cols_ref[b]
        src = pl.ds(pl.multiple_of(c * blk, blk), blk)
        for g in range(pairs):
            at = slice(g * LANES, (g + 1) * LANES)
            cot = grad_ref[r, at]
            left = jnp.concatenate([cot, centre[r, :]], axis=1)
            right = jnp.concatenate(
                [both(proj_src[src, at]), (-pick(g, True)).astype(BF16)], axis=1
            )
            apart = mm(left, right, 1, 1)
            shares, grads, sums = [], [], []
            for q in range(2):
                h = 2 * g + q
                share = weights[b, h] * inv_wide[h, r, :]
                grad = share * apart[:, q * blk : (q + 1) * blk] * slopes[b, h]
                sums.append(jnp.sum(grad, axis=0, keepdims=True))
                shares.append(share.astype(BF16))
                grads.append(grad.astype(BF16))
            grad_score_src[c, 2 * g : 2 * g + 2, :] += jnp.concatenate(sums, axis=0)
            grad_score_dst[r, :] += mm(
                jnp.concatenate(grads, axis=1), pick(g, False).astype(BF16)
            )
            grad_source[src, at] += mm(jnp.concatenate(shares, axis=0), both(cot), 0, 0)
        return carry

    lax.fori_loop(0, count, backward, 0)

    score_grad = grad_score_dst[...] + self_grad
    self_grad_b = self_grad.astype(BF16)
    score_grad_b = score_grad.astype(BF16)
    flat = (
        mm_split(self_att, ones_heads, 2) * cotan
        + mm(self_grad_b, tall_src.astype(BF16))
        + mm(score_grad_b, tall_dst.astype(BF16))
    ).astype(BF16)
    grad_dst_ref[...] = mm(flat, weight_ref[...], 1, 1)
    part_weight = mm(x_dst_ref[...], flat, 0, 0)
    att_src_part = mm(self_grad_b, proj_dst[...], 0, 0)[:heads]
    att_dst_part = mm(score_grad_b, proj_dst[...], 0, 0)[:heads]

    spread_b = spread_src.astype(BF16)
    for s in range(source_blocks):
        at = slice(s * blk, (s + 1) * blk)
        scores = grad_score_src[s].astype(BF16)
        source = (grad_source[at, :] + mm(scores, spread_b, 0, 0)).astype(BF16)
        part_src_ref[at, :] = mm(source, weight_ref[...], 1, 1).astype(part_src_ref.dtype)
        part_weight += mm(x_all_ref[at, :], source, 0, 0)
        att_src_part += mm(scores, proj_src[at, :])
    for g in range(pairs):
        part_weight_ref[g * inputs : (g + 1) * inputs, :] = part_weight[
            :, g * LANES : (g + 1) * LANES
        ].astype(part_weight_ref.dtype)
    src_row = jnp.sum(jnp.where(own, att_src_part, 0.0), axis=0, keepdims=True)
    dst_row = jnp.sum(jnp.where(own, att_dst_part, 0.0), axis=0, keepdims=True)
    stack = [row[:, g * LANES : (g + 1) * LANES] for row in (src_row, dst_row) for g in range(pairs)]
    att = jnp.concatenate(stack, axis=0)
    part_att_ref[...] = jnp.concatenate(
        [att.astype(BF16).astype(F32), att - att.astype(BF16).astype(F32)], axis=0
    ).astype(part_att_ref.dtype)


def layer(x_all, x_dst, weight, att_src, att_dst, grad_out, rows, cols, masks, counts):
    heads = att_src.shape[0]
    inputs, width = weight.shape
    slots, blk = masks.shape[:2]
    sources, dest = x_all.shape[0], x_dst.shape[0]
    blocks = sources // blk
    vmem = pl.BlockSpec(memory_space=pltpu.VMEM)
    smem = pl.BlockSpec(memory_space=pltpu.SMEM)
    return pl.pallas_call(
        layer_kernel,
        out_shape=(
            jax.ShapeDtypeStruct((dest, inputs), F32),
            jax.ShapeDtypeStruct((sources, inputs), BF16),
            jax.ShapeDtypeStruct((width // LANES * inputs, LANES), BF16),
            jax.ShapeDtypeStruct((16, LANES), BF16),
        ),
        in_specs=[smem] * 3 + [vmem] * 7,
        out_specs=(vmem,) * 4,
        scratch_shapes=[
            pltpu.VMEM((sources, width), BF16),
            pltpu.VMEM((dest, width), BF16),
            pltpu.VMEM((blocks, heads, blk), F32),
            pltpu.VMEM((heads, dest, LANES), F32),
            pltpu.VMEM((heads, dest, LANES), F32),
            pltpu.VMEM((slots, heads, blk, blk), F32),
            pltpu.VMEM((slots, heads, blk, blk), F32),
            pltpu.VMEM((dest, width), F32),
            pltpu.VMEM((dest, LANES), F32),
            pltpu.VMEM((dest, LANES), BF16),
            pltpu.VMEM((sources, width), F32),
            pltpu.VMEM((blocks, heads, blk), F32),
            pltpu.VMEM((dest, LANES), F32),
        ],
        compiler_params=pltpu.CompilerParams(vmem_limit_bytes=52 * 1024 * 1024),
    )(rows, cols, counts, x_all, x_dst, weight, att_src, att_dst, grad_out, masks)


def unpack_weight(part, inputs):
    pieces = part.shape[0] // inputs
    return jnp.concatenate([part[g * inputs : (g + 1) * inputs] for g in range(pieces)], axis=1)


def shards(
    x_src, x_dst, weight, att_src, att_dst, grad_out, block_rows, block_cols, block_masks, block_counts
):
    heads, head_dim = att_src.shape
    x_all = lax.all_gather(x_src, "panel", axis=0, tiled=True)
    grad_dst, part_src, part_weight, part_att = layer(
        x_all, x_dst, weight, att_src, att_dst, grad_out, block_rows, block_cols, block_masks, block_counts
    )
    share = lax.psum_scatter(part_src.astype(F32), "panel", scatter_dimension=0, tiled=True)
    att = part_att[:8].astype(F32) + part_att[8:].astype(F32)
    grad_src = lax.psum(share, "rep")
    grad_weight, att = lax.psum(
        (unpack_weight(part_weight, weight.shape[0]).astype(F32), att), ("panel", "rep")
    )
    att = att.reshape(2, heads, head_dim)
    return grad_src, grad_dst, grad_weight, att[0], att[1]


def solution(mesh):
    both = P(("panel", "rep"))
    return jax.shard_map(
        shards,
        mesh=mesh,
        in_specs=(P("panel", None), both, P(), P(), P(), both, both, both, both, both),
        out_specs=(P("panel", None), both, P(), P(), P()),
        check_vma=False,
    )
```

time: 386 us -> 230 us (0.60)
  waiting for transfers between devices: 220 us -> 113 us
  matrix products: 66.7 us -> 0 us
  blocking collectives: 39.7 us -> 80.2 us
  local copies, waits for them, and re-layouts: 25.1 us -> 6.32 us
  other arithmetic: 18.6 us -> 1.76 us
  Pallas kernels: 0 us -> 12.8 us
    dot_general x24 -> x0, matrix products: 66.7 us -> none  [the longest x1 15.5 us: backward_group(): jnp.einsum('gihk,gjhk->ghij', cotan_rows, source_rows, preferred_element_...]
    reduce_scatter x1, waiting for transfers between devices: 62.2 us -> 17.4 us  [shards(): lax.psum_scatter(part_src.astype(F32), 'panel', scatter_dimension=0, tile...]
    all_gather x1 -> x0, waiting for transfers between devices: 34.4 us -> none  [shards(): proj_all = lax.all_gather(proj_own, 'panel', axis=0, tiled=True)]
    psum x2, waiting for transfers between devices: 123 us -> 95.1 us  [the longest x1 73.4 us: shards(): lax.psum((unpack_weight(part_weight, weight.shape[0]).astype(F32), att),...]
    all_gather x0 -> x1, blocking collectives: none -> 24.9 us  [shards(): x_all = lax.all_gather(x_src, 'panel', axis=0, tiled=True)]
    psum x1, blocking collectives: 39.7 us -> 55.3 us  [shards(): lax.psum((unpack_weight(part_weight, weight.shape[0]).astype(F32), att),...]
    pallas_call x0 -> x1, Pallas kernels: none -> 12.8 us  [layer(): pl.pallas_call(layer_kernel, out_shape=(jax.ShapeDtypeStruct((dest, input...]
    reduce_sum x2 -> x0, other arithmetic: 11.2 us -> none  [the longest x1 9.62 us: forward_group(): edge_weight.sum(axis=3)]
  transfers between devices with their start and end apart: 4 -> 3, of which waited for: 3 -> 3; matrix products, arithmetic and copies ran while one was open for 6% -> 1% of each run, Pallas kernels for 0% -> 0%
where the time goes in v1:
time: 230 us
  waiting for transfers between devices  113 us (49%)
  blocking collectives  80.2 us (35%)
  between operations  16.3 us (7%)
  Pallas kernels  12.8 us (6%)
  local copies, waits for them, and re-layouts  6.32 us (3%)
    psum x1, waiting for transfers between devices, shards(): lax.psum((unpack_weight(part_weight, weight.shape[0]).astype(F32), att),...  73.4 us
    psum x1, blocking collectives, shards(): lax.psum((unpack_weight(part_weight, weight.shape[0]).astype(F32), att),...  55.3 us
    all_gather x1, blocking collectives, shards(): x_all = lax.all_gather(x_src, 'panel', axis=0, tiled=True)  24.9 us
    psum x1, waiting for transfers between devices, shards(): grad_src = lax.psum(share, 'rep')  21.8 us
    reduce_scatter x1, waiting for transfers between devices, shards(): lax.psum_scatter(part_src.astype(F32), 'panel', scatter_dimension=0, tile...  17.4 us
    pallas_call x1, Pallas kernels, layer(): pl.pallas_call(layer_kernel, out_shape=(jax.ShapeDtypeStruct((dest, input...  12.8 us
    unnamed x16, local copies, waits for them, and re-layouts  4.97 us
  transfers between devices with their start and end apart: 3, of which 3 were waited for; matrix products, arithmetic and copies ran while one was open for 1% of the time, Pallas kernels for 0%

profile of v1, /device:TPU:0, one launch (start us, length us, event | category | flops | bytes accessed | tf_op | source)
XLA Modules:
  0.0 230.1 jit_solution(3720564508246961802)
XLA Ops:
  8.0 0.0 copy-start
  8.0 0.0 reduce-scatter.2.cloned.1.call-start
  8.8 0.0 copy-start.3
  8.8 0.0 copy-start.4
  8.8 0.0 copy-start.5
  8.8 0.0 copy-start.6
  8.8 24.9 %all_gather.3.x_all_ref = bf16[2048,128]{1,0:T(8,128)(2,1)S(1)} all-gather(bf16[128,128]{1,0:T(8,128)(2,1)} %param.10), channel_id=1, replica_groups=mesh['panel'=16,'rep'=2] {'panel'}, dimensions={0}, use_global_device_ids=true | all-gather | bytes 557056 | tf_op jit(solution)/shard_map/all_gather | solution.py:254
  33.7 0.0 copy-done
  33.7 0.0 copy-done.3
  33.7 0.0 copy-done.4
  33.7 0.0 copy-done.5
  33.7 0.0 copy-done.6
  33.8 0.0 copy-start.1
  33.8 0.9 copy-done.1
  34.7 0.0 copy-start.2
  34.7 0.9 copy-done.2
  35.6 12.8 %shard_map.137 = (f32[512,128]{1,0:T(8,128)}, bf16[2048,128]{1,0:T(8,128)(2,1)S(1)}, bf16[512,128]{1,0:T(8,128)(2,1)S(1)}, bf16[16,128]{1,0:T(8,128)(2,1)S(1)}) custom-call(s32[16]{0:T(128)S(1)} %copy-done.5, s32[16]{0:T(128)S(1)} %copy-done.6, s32[1]{0:T(128)S(6)} %copy.17.count_ref, bf16[2048,128]{1,0:T(8,128)(2,1)S(1)} %all_gather.3.x_all_ref, ...), custom_call_target="tpu_custom_call" | custom-call | tf_op jit(solution)/shard_map/pallas_call | solution.py:216
  48.4 1.0 convert_element_type.12
  49.4 0.0 reduce-scatter.2.cloned.1.call-update
  49.5 0.0 all-reduce.5.cloned.1.call-start
  49.5 0.7 maximum_convert_fusion
  50.3 0.0 all-reduce.5.cloned.1.call-update
  50.3 0.0 all-reduce.3.cloned.1.call-start
  50.3 55.3 %psum.23 = f32[8,128]{1,0:T(8,128)S(1)} all-reduce(f32[8,128]{1,0:T(8,128)S(1)} %convert_add_fusion), channel_id=1, replica_groups=mesh['panel'=16,'rep'=2] {'panel','rep'}, use_global_device_ids=true, to_apply=%region_3.0 | all-reduce | flops 1024 | bytes 8192 | tf_op jit(solution)/shard_map/psum | solution.py:261
  105.6 17.4 %reduce-scatter.2.cloned.1.call-done = f32[128,128]{1,0:T(8,128)} async-done(((f32[2048,128]{1,0:T(8,128)}), f32[128,128]{1,0:T(8,128)}) %reduce-scatter.2.cloned.1.call-update) | async-done | bytes 65552 | tf_op jit(solution)/shard_map/reduce_scatter | solution.py:258
  123.0 0.0 all-reduce.3.cloned.1.call-update
  123.0 0.7 squeeze.6
  123.7 0.7 squeeze.7
  124.4 73.4 %all-reduce.5.cloned.1.call-done = f32[128,512]{1,0:T(8,128)} async-done(((f32[128,512]{1,0:T(8,128)}), f32[128,512]{1,0:T(8,128)}) %all-reduce.5.cloned.1.call-update) | async-done | bytes 262160 | tf_op jit(solution)/shard_map/psum | solution.py:261
  197.7 21.8 %all-reduce.3.cloned.1.call-done = f32[128,128]{1,0:T(8,128)} async-done(((f32[128,128]{1,0:T(8,128)}), f32[128,128]{1,0:T(8,128)}) %all-reduce.3.cloned.1.call-update) | async-done | bytes 65552 | tf_op jit(solution)/shard_map/psum | solution.py:260
  219.5 1.5 copy.18
  221.0 1.7 copy.19
  (3 shorter events, 0.0 us)
Async XLA Ops:
  8.0 25.7 %copy-start = (bf16[512,512]{1,0:T(8,128)(2,1)S(1)}, bf16[512,512]{1,0:T(8,128)(2,1)}, u32[]{:S(2)}) copy-start(bf16[512,512]{1,0:T(8,128)(2,1)} %grad_ref.1) | copy-start | bytes 1572868
  8.0 115.0 %reduce-scatter.2.cloned.1.call-start = ((), (), s32[]{:S(2)}) async-start(), calls=%async_computation.1 | async-start | bytes 1114112 | tf_op jit(solution)/shard_map/reduce_scatter | solution.py:258
  8.8 25.0 %copy-start.3 = (f32[8,64]{1,0:T(8,128)S(1)}, f32[8,64]{1,0:T(8,128)}, u32[]{:S(2)}) copy-start(f32[8,64]{1,0:T(8,128)} %att_src_ref.1) | copy-start | bytes 6148
  8.8 25.0 %copy-start.4 = (f32[8,64]{1,0:T(8,128)S(1)}, f32[8,64]{1,0:T(8,128)}, u32[]{:S(2)}) copy-start(f32[8,64]{1,0:T(8,128)} %att_dst_ref.1) | copy-start | bytes 6148
  8.8 25.0 %copy-start.5 = (s32[16]{0:T(128)S(1)}, s32[16]{0:T(128)}, u32[]{:S(2)}) copy-start(s32[16]{0:T(128)} %rows_ref.1) | copy-start | bytes 196
  8.8 25.0 %copy-start.6 = (s32[16]{0:T(128)S(1)}, s32[16]{0:T(128)}, u32[]{:S(2)}) copy-start(s32[16]{0:T(128)} %cols_ref.1) | copy-start | bytes 196
  33.8 0.9 copy-start.1
  34.7 0.9 copy-start.2
  49.5 148.3 %all-reduce.5.cloned.1.call-start = ((), (), s32[]{:S(2)}) async-start(), calls=%async_computation.3 | async-start | bytes 524288 | tf_op jit(solution)/shard_map/psum | solution.py:261
  50.3 169.2 %all-reduce.3.cloned.1.call-start = ((), (), s32[]{:S(2)}) async-start(), calls=%async_computation.2 | async-start | bytes 131072 | tf_op jit(solution)/shard_map/psum | solution.py:260
Sparse Core Ops, SparseCore 0:
  49.6 73.3 reduce-scatter.1
Sparse Core Ops, SparseCore 1:
  56.0 141.7 all-reduce.4
  199.9 19.5 all-reduce.2
